TPU v7x, 32 devices: a whole 2x2x4 slice. The times are simulated.
32 devices in a mesh: layer: 4 (over x, core), feat: 8 (over z, y).
Axes of the slice: x: 2, y: 2, z: 4, core: 2. Of those that a mesh axis runs over, the one named last changes fastest.
Arguments:
- sources: bfloat16 [4, 512, 4096], P('layer', 'feat'), may hold values from -6 to 6
- targets: bfloat16 [4, 512, 4096], P('layer', 'feat'), may hold values from -6 to 6
- enc_weight: bfloat16 [4, 8192, 4096], P('layer', 'feat'), may hold values from -0.09375 to 0.09375
- dec_weight: bfloat16 [4, 4, 8192, 4096], P('layer', None, 'feat'), may hold values from -0.0625 to 0.0625
- active: int32 [4, 8192, 512], P('layer', 'feat'), may hold values 0 or 1
Outputs:
- errors: float32 [4, 512, 4096], P('layer', 'feat')
- grad_dec: bfloat16 [4, 4, 8192, 4096], P('layer', None, 'feat')
- grad_enc: bfloat16 [4, 8192, 4096], P('layer', 'feat')
All inputs are finite; a program needn't handle non-finite values. No bound on the sum of `active` on one device may be relied on, other than what follows from the above.
Results may differ from a plain program's by a relative error of at most 0.0061.
Values may be sent and summed in bfloat16 or wider, within the bound.
A program may use at most 192 MiB of HBM per device.

v0:
```python
import math

import jax
import jax.numpy as jnp
from jax import lax
from jax.sharding import PartitionSpec as P

TOKENS = 512


def on_device(sources, targets, enc_weight, dec_weight, active):
    per_group = sources.shape[0]
    layer_count = dec_weight.shape[1]
    group_index = lax.axis_index("layer")
    source_full = lax.all_gather(sources, "feat", axis=1, tiled=True)
    pre_acts = jnp.einsum(
        "sfd,std->sft", enc_weight, source_full, preferred_element_type=jnp.float32
    )
    features = (active.astype(jnp.float32) * pre_acts).astype(jnp.bfloat16)
    all_features = lax.all_gather(features, "layer", axis=0, tiled=True)
    target_pos = group_index * per_group + jnp.arange(per_group, dtype=jnp.int32)
    source_pos = jnp.arange(layer_count, dtype=jnp.int32)
    causal = source_pos[None, :] <= target_pos[:, None]
    masked = all_features[None] * causal[:, :, None, None].astype(jnp.bfloat16)
    recon_terms = jnp.einsum(
        "slft,slfd->std", masked, dec_weight, preferred_element_type=jnp.float32
    )
    scale = 1.0 / math.sqrt(TOKENS)
    recon_sum = lax.psum_scatter(recon_terms, "feat", scatter_dimension=1, tiled=True)
    errors = recon_sum - targets.astype(jnp.float32)
    scaled_error = (errors * scale).astype(jnp.bfloat16)
    scaled_full = lax.all_gather(scaled_error, "feat", axis=1, tiled=True)
    grad_dec = jnp.einsum(
        "slft,std->slfd", masked, scaled_full, preferred_element_type=jnp.float32
    ).astype(jnp.bfloat16)
    partial_grad = jnp.einsum(
        "slfd,std->slft", dec_weight, scaled_full, preferred_element_type=jnp.float32
    )
    partial_grad = jnp.sum(partial_grad * causal[:, :, None, None].astype(jnp.float32), axis=0)
    feature_grad = lax.psum_scatter(partial_grad, "layer", scatter_dimension=0, tiled=True)
    pre_grad = (active.astype(jnp.float32) * feature_grad).astype(jnp.bfloat16)
    grad_enc = jnp.einsum(
        "sft,std->sfd", pre_grad, source_full, preferred_element_type=jnp.float32
    ).astype(jnp.bfloat16)
    return (errors, grad_dec, grad_enc)


def solution(mesh):
    in_specs = (
        P("layer", "feat", None),
        P("layer", "feat", None),
        P("layer", "feat", None),
        P("layer", None, "feat", None),
        P("layer", "feat", None),
    )
    out_specs = (P("layer", "feat", None), P("layer", None, "feat", None), P("layer", "feat", None))
    return jax.shard_map(
        on_device, mesh=mesh, in_specs=in_specs, out_specs=out_specs, check_vma=False
    )
```

profile of v0, /device:TPU:0, one launch (start us, length us, event | category | flops | bytes accessed | tf_op | source)
XLA Modules:
  0.0 490.0 jit_solution(13013433915122301063)
XLA Ops:
  7.2 0.0 all-gather.4.cloned.1.call-start
  7.2 0.7 all-gather.4.cloned.1.call-update
  7.9 0.0 all-gather.6.cloned.1.call-start
  7.9 78.3 %all-gather.4.cloned.1.call-done = bf16[1,512,4096]{2,1,0:T(8,128)(2,1)} async-done(((bf16[1,64,4096]{2,1,0:T(8,128)(2,1)}), bf16[1,512,4096]{2,1,0:T(8,128)(2,1)}) %all-gather.4.cloned.1.call-update) | async-done | bytes 4194320 | tf_op jit(solution)/shard_map/all_gather | solution.py:15
  86.3 10.7 %fusion.15 = bf16[1,1024,512]{2,1,0:T(8,128)(2,1)} fusion(s32[1,1024,512]{2,1,0:T(8,128)} %param.9, bf16[1,512,4096]{2,1,0:T(8,128)(2,1)} %all-gather.4.cloned.1.call-done, bf16[1,1024,4096]{2,1,0:T(8,128)(2,1)} %param.7), kind=kOutput, calls=%fused_computation.17 | convolution fusion | flops 4296540160 | bytes 15728640 | tf_op jit(solution)/shard_map/sfd,std->sft/dot_general | solution.py:16
  97.0 0.0 all-gather.6.cloned.1.call-update
  97.0 0.0 reduce-scatter.3.cloned.1.call-start
  97.1 32.8 %all-gather.6.cloned.1.call-done = bf16[4,1024,512]{2,1,0:T(8,128)(2,1)} async-done(((bf16[1,1024,512]{2,1,0:T(8,128)(2,1)}), bf16[4,1024,512]{2,1,0:T(8,128)(2,1)}) %all-gather.6.cloned.1.call-update) | async-done | bytes 4194320 | tf_op jit(solution)/shard_map/all_gather | solution.py:20
  129.9 24.3 %fusion.6 = f32[1,512,4096]{2,1,0:T(8,128)} fusion(bf16[1,4,1024,4096]{3,2,1,0:T(8,128)(2,1)} %param.8, bf16[4,1024,512]{2,1,0:T(8,128)(2,1)} %all-gather.6.cloned.1.call-done, bf16[4]{0:T(256)(128)(2,1)S(1)} %compare_convert_fusion.1), kind=kOutput, calls=%fused_computation.9 | convolution fusion | flops 17181966336 | bytes 46137352 | tf_op jit(solution)/shard_map/slft,slfd->std/dot_general | solution.py:25
  154.2 0.0 copy-start
  154.2 0.0 reduce-scatter.3.cloned.1.call-update
  154.3 0.0 all-gather.8.cloned.1.call-start
  154.3 149.1 %reduce-scatter.3.cloned.1.call-done = f32[1,64,4096]{2,1,0:T(8,128)} async-done(((f32[1,512,4096]{2,1,0:T(8,128)}), f32[1,64,4096]{2,1,0:T(8,128)}) %reduce-scatter.3.cloned.1.call-update) | async-done | bytes 1048592 | tf_op jit(solution)/shard_map/reduce_scatter | solution.py:29
  303.4 0.0 copy-done
  303.4 2.5 multiply_convert_fusion.1
  305.9 0.0 all-gather.8.cloned.1.call-update
  305.9 0.2 reduce-scatter.5.cloned.1.call-start
  306.2 72.4 %all-gather.8.cloned.1.call-done = bf16[1,512,4096]{2,1,0:T(8,128)(2,1)} async-done(((bf16[1,64,4096]{2,1,0:T(8,128)(2,1)}), bf16[1,512,4096]{2,1,0:T(8,128)(2,1)}) %all-gather.8.cloned.1.call-update) | async-done | bytes 4194320 | tf_op jit(solution)/shard_map/all_gather | solution.py:32
  378.6 24.0 %multiply_bitcast_fusion = f32[4,1024,512]{2,1,0:T(8,128)} fusion(f32[4]{0:T(128)S(1)} %compare_convert_fusion, bf16[1,4,1024,4096]{3,2,1,0:T(8,128)(2,1)} %param.8, bf16[1,512,4096]{2,1,0:T(8,128)(2,1)} %all-gather.8.cloned.1.call-done), kind=kOutput, calls=%fused_computation.8 | convolution fusion | flops 17181966336 | bytes 46137360 | tf_op jit(solution)/shard_map/slfd,std->slft/dot_general | solution.py:36
  402.6 0.0 reduce-scatter.5.cloned.1.call-update
  402.7 0.0 copy-start.1
  402.7 25.3 %convert_bitcast_fusion = bf16[1,4,1024,4096]{3,2,1,0:T(8,128)(2,1)} fusion(bf16[1,512,4096]{2,1,0:T(8,128)(2,1)} %all-gather.8.cloned.1.call-done, bf16[4,1024,512]{2,1,0:T(8,128)(2,1)} %all-gather.6.cloned.1.call-done, bf16[4]{0:T(256)(128)(2,1)S(1)} %compare_convert_fusion.1), kind=kOutput, calls=%fused_computation.4 | convolution fusion | flops 17198743552 | bytes 41943048 | tf_op jit(solution)/shard_map/slft,std->slfd/dot_general | solution.py:33
  428.0 44.8 %reduce-scatter.5.cloned.1.call-done = f32[1,1024,512]{2,1,0:T(8,128)} async-done(((f32[4,1024,512]{2,1,0:T(8,128)}), f32[1,1024,512]{2,1,0:T(8,128)}) %reduce-scatter.5.cloned.1.call-update) | async-done | bytes 2097168 | tf_op jit(solution)/shard_map/reduce_scatter | solution.py:40
  472.8 0.0 copy-done.1
  472.8 10.7 %convert_bitcast_fusion.1 = bf16[1,1024,4096]{2,1,0:T(8,128)(2,1)} fusion(bf16[1,512,4096]{2,1,0:T(8,128)(2,1)} %all-gather.4.cloned.1.call-done, f32[1,1024,512]{2,1,0:T(8,128)} %reduce-scatter.5.cloned.1.call-done, s32[1,1024,512]{2,1,0:T(8,128)S(1)} %copy-done.1), kind=kOutput, calls=%fused_computation.7 | convolution fusion | flops 4300734464 | bytes 16777216 | tf_op jit(solution)/shard_map/sft,std->sfd/dot_general | solution.py:42
  (2 shorter events, 0.0 us)
Async XLA Ops:
  7.2 79.1 %all-gather.4.cloned.1.call-start = ((), (), s32[]{:S(2)}) async-start(), calls=%async_computation.2 | async-start | bytes 4718592 | tf_op jit(solution)/shard_map/all_gather | solution.py:15
  7.9 122.0 %all-gather.6.cloned.1.call-start = ((), (), s32[]{:S(2)}) async-start(), calls=%async_computation.3 | async-start | bytes 5242880 | tf_op jit(solution)/shard_map/all_gather | solution.py:20
  97.0 206.4 %reduce-scatter.3.cloned.1.call-start = ((), (), s32[]{:S(2)}) async-start(), calls=%async_computation.4 | async-start | bytes 9437184 | tf_op jit(solution)/shard_map/reduce_scatter | solution.py:29
  154.2 149.1 %copy-start = (bf16[1,64,4096]{2,1,0:T(8,128)(2,1)S(1)}, bf16[1,64,4096]{2,1,0:T(8,128)(2,1)}, u32[]{:S(2)}) copy-start(bf16[1,64,4096]{2,1,0:T(8,128)(2,1)} %param.6) | copy-start | bytes 1572868
  154.3 224.3 %all-gather.8.cloned.1.call-start = ((), (), s32[]{:S(2)}) async-start(), calls=%async_computation.5 | async-start | bytes 4718592 | tf_op jit(solution)/shard_map/all_gather | solution.py:32
  305.9 166.8 %reduce-scatter.5.cloned.1.call-start = ((), (), s32[]{:S(2)}) async-start(), calls=%async_computation.6 | async-start | bytes 10485760 | tf_op jit(solution)/shard_map/reduce_scatter | solution.py:40
  402.7 70.1 %copy-start.1 = (s32[1,1024,512]{2,1,0:T(8,128)S(1)}, s32[1,1024,512]{2,1,0:T(8,128)}, u32[]{:S(2)}) copy-start(s32[1,1024,512]{2,1,0:T(8,128)} %param.9) | copy-start | bytes 6291460
Sparse Core Ops, SparseCore 0:
  10.1 76.0 all-gather.3
  97.1 32.7 all-gather.5
  154.4 148.9 reduce-scatter.2
  306.2 72.3 all-gather.7
  402.8 69.9 reduce-scatter.4
where the time goes:
time: 490 us
  waiting for transfers between devices  378 us (77%)
  matrix products  95.1 us (19%)
  between operations  13.8 us (3%)
    reduce_scatter x1, waiting for transfers between devices, on_device(): lax.psum_scatter(recon_terms, 'feat', scatter_dimension=1, tiled=True)  149 us
    all_gather x1, waiting for transfers between devices, on_device(): source_full = lax.all_gather(sources, 'feat', axis=1, tiled=True)  78.3 us
    all_gather x1, waiting for transfers between devices, on_device(): scaled_full = lax.all_gather(scaled_error, 'feat', axis=1, tiled=True)  72.4 us
    reduce_scatter x1, waiting for transfers between devices, on_device(): lax.psum_scatter(partial_grad, 'layer', scatter_dimension=0, tiled=True)  44.8 us
    all_gather x1, waiting for transfers between devices, on_device(): all_features = lax.all_gather(features, 'layer', axis=0, tiled=True)  32.8 us
    dot_general x1, matrix products, on_device(): jnp.einsum('slft,std->slfd', masked, scaled_full, preferred_element_type=...  25.3 us
    dot_general x1, matrix products, on_device(): jnp.einsum('slft,slfd->std', masked, dec_weight, preferred_element_type=j...  24.3 us
    dot_general x1, matrix products, on_device(): jnp.einsum('slfd,std->slft', dec_weight, scaled_full, preferred_element_t...  24 us
  transfers between devices with their start and end apart: 5, of which 5 were waited for; matrix products, arithmetic and copies ran while one was open for 5% of the time, Pallas kernels for 0%

commit v1 on v0

v1 whole, which is shorter than its diff:
```python
import functools
import math

import jax
import jax.numpy as jnp
from jax import lax
from jax.experimental import pallas as pl
from jax.experimental.pallas import tpu as pltpu
from jax.sharding import PartitionSpec as P

MESH = pl.DeviceIdType.MESH
VMEM_LIMIT = 40 * 1024 * 1024


def place(axis, count):
    me = lax.axis_index(axis)
    return me, me // 2, lax.rem(me, 2), count // 2


def greet(axis, count):
    me, z, y, length = place(axis, count)
    barrier = pltpu.get_barrier_semaphore()

    def signal(device):
        pl.semaphore_signal(barrier, inc=1, device_id={axis: device}, device_id_type=MESH)

    signal(me + 1 - 2 * y)
    pl.when(z > 0)(lambda: signal(me - 2))
    pl.when(z < length - 1)(lambda: signal(me + 2))
    pl.semaphore_wait(barrier, 1 + (z > 0).astype(jnp.int32) + (z < length - 1).astype(jnp.int32))


def gather(axis, count, causal, own, out, line_sem, side_sem, recv_sem):
    me, z, y, length = place(axis, count)
    other = 1 - y

    def copy(block, source, device, sem):
        return pltpu.make_async_remote_copy(
            src_ref=source, dst_ref=out.at[block], send_sem=sem, recv_sem=recv_sem.at[block],
            device_id={axis: device}, device_id_type=MESH)

    def across(line, source):
        return copy(line * 2 + y, source, z * 2 + other, side_sem.at[line])

    def right(line, source):
        return copy(line * 2 + y, source, me + 2, line_sem.at[0, line])

    def left(line, source):
        return copy(line * 2 + y, source, me - 2, line_sem.at[1, line])

    def arrived(block):
        copy(block, own, me, side_sem.at[0]).wait_recv()

    def own_across():
        return (y == 0) if causal else (y >= 0)

    pl.when(z < length - 1)(lambda: right(z, own).start())
    if not causal:
        pl.when(z > 0)(lambda: left(z, own).start())
    pl.when(own_across())(lambda: across(z, own).start())
    for step in range(1, length):
        @pl.when(z - step >= 0)
        def _():
            line = z - step
            block = line * 2 + y
            arrived(block)
            pl.when(z < length - 1)(lambda: right(line, out.at[block]).start())
            across(line, out.at[block]).start()

        if not causal:
            @pl.when(z + step < length)
            def _():
                line = z + step
                block = line * 2 + y
                arrived(block)
                pl.when(z > 0)(lambda: left(line, out.at[block]).start())
                across(line, out.at[block]).start()

    for line in range(length):
        @pl.when((line < z) | ((line == z) & (y == 1)) if causal else (z >= 0))
        def _():
            arrived(line * 2 + other)

        @pl.when((line < z) | ((line == z) & (y == 0)) if causal else (z >= 0))
        def _():
            across(line, own).wait_send()

        pl.when((line <= z) & (z < length - 1))(lambda: right(line, own).wait_send())
        if not causal:
            pl.when((line >= z) & (z > 0))(lambda: left(line, own).wait_send())


def gather_sems(count):
    return [
        pltpu.SemaphoreType.DMA((2, count // 2)),
        pltpu.SemaphoreType.DMA((count // 2,)),
        pltpu.SemaphoreType.DMA((count,)),
    ]


def gather_kernel(axis, count, causal, own, out, local_sem, line_sem, side_sem, recv_sem):
    me = lax.axis_index(axis)
    local = pltpu.make_async_copy(own, out.at[me], local_sem)
    local.start()
    greet(axis, count)
    gather(axis, count, causal, own, out, line_sem, side_sem, recv_sem)
    local.wait()


def gather_call(block, axis, causal, collective_id):
    count = lax.axis_size(axis)
    return pl.pallas_call(
        functools.partial(gather_kernel, axis, count, causal),
        out_shape=jax.ShapeDtypeStruct((count,) + block.shape, block.dtype),
        in_specs=[pl.BlockSpec(memory_space=pl.ANY)],
        out_specs=pl.BlockSpec(memory_space=pl.ANY),
        scratch_shapes=[pltpu.SemaphoreType.DMA(())] + gather_sems(count),
        compiler_params=pltpu.CompilerParams(collective_id=collective_id, has_side_effects=True),
    )(block)


def reduce_kernel(
    axis, count, scale, parts, targets, errors, full,
    from_side, from_left, from_right, to_right, to_left, scaled,
    local_sem, line_sem, side_sem, recv_sem,
    side_send, side_recv, right_send, right_recv, left_send, left_recv,
):
    me, z, y, length = place(axis, count)
    rows = targets.shape[0]
    step_rows = min(16, rows)
    greet(axis, count)

    def copy(source, target, send_sem, recv, device):
        return pltpu.make_async_remote_copy(
            src_ref=source, dst_ref=target, send_sem=send_sem, recv_sem=recv,
            device_id={axis: device}, device_id_type=MESH)

    def side(line):
        return copy(parts.at[line * 2 + 1 - y], from_side.at[line], side_send.at[line],
                    side_recv.at[line], me + 1 - 2 * y)

    def right(line):
        return copy(to_right.at[line], from_left.at[line], right_send.at[line],
                    right_recv.at[line], me + 2)

    def left(line):
        return copy(to_left.at[line], from_right.at[line], left_send.at[line],
                    left_recv.at[line], me - 2)

    for step in range(length - 1):
        pl.when(length - 1 - step > z)(lambda: side(length - 1 - step).start())
        pl.when(step < z)(lambda: side(step).start())
    side(z).start()

    def add(line, others, store):
        @pl.loop(0, rows // step_rows)
        def _(index):
            at = pl.ds(pl.multiple_of(index * step_rows, step_rows), step_rows)
            total = parts[line * 2 + y, at, :].astype(jnp.float32)
            for ref in others:
                total += ref[line, at, :].astype(jnp.float32)
            store(at, total)

    def pass_on(line, incoming, has_incoming, outgoing, message, recv):
        def store(at, total):
            outgoing[line, at, :] = total.astype(outgoing.dtype)

        side(line).wait_recv()

        @pl.when(has_incoming)
        def _():
            recv(line).wait_recv()
            add(line, (from_side, incoming), store)

        @pl.when(jnp.logical_not(has_incoming))
        def _():
            add(line, (from_side,), store)

        message(line).start()

    for step in range(length - 1):
        @pl.when(length - 1 - step > z)
        def _():
            pass_on(length - 1 - step, from_left, z > 0, to_right, right, right)

        @pl.when(step < z)
        def _():
            pass_on(step, from_right, z < length - 1, to_left, left, left)

    side(z).wait_recv()

    def finish(others):
        def store(at, total):
            error = total - targets[at, :].astype(jnp.float32)
            errors[at, :] = error
            scaled[at, :] = (error * scale).astype(scaled.dtype)

        add(z, others, store)

    @pl.when(z > 0)
    def _():
        right(z).wait_recv()

    @pl.when(z < length - 1)
    def _():
        left(z).wait_recv()

    pl.when((z > 0) & (z < length - 1))(lambda: finish((from_side, from_left, from_right)))
    pl.when((z > 0) & (z == length - 1))(lambda: finish((from_side, from_left)))
    pl.when((z == 0) & (z < length - 1))(lambda: finish((from_side, from_right)))
    pl.when((z == 0) & (z == length - 1))(lambda: finish((from_side,)))

    local = pltpu.make_async_copy(scaled, full.at[me], local_sem)
    local.start()
    gather(axis, count, False, scaled, full, line_sem, side_sem, recv_sem)
    local.wait()
    for line in range(length):
        side(line).wait_send()
        pl.when(line > z)(lambda: right(line).wait_send())
        pl.when(line < z)(lambda: left(line).wait_send())


def reduce_call(parts, targets, axis, scale, collective_id):
    count, rows, width = parts.shape
    length = count // 2
    lane = pltpu.VMEM((length, rows, width), parts.dtype)
    sems = pltpu.SemaphoreType.DMA((length,))
    vmem = pl.BlockSpec(memory_space=pltpu.VMEM)
    return pl.pallas_call(
        functools.partial(reduce_kernel, axis, count, scale),
        out_shape=(
            jax.ShapeDtypeStruct((rows, width), jnp.float32),
            jax.ShapeDtypeStruct((count, rows, width), parts.dtype),
        ),
        in_specs=[vmem, vmem],
        out_specs=(vmem, pl.BlockSpec(memory_space=pl.ANY)),
        scratch_shapes=[lane] * 5 + [pltpu.VMEM((rows, width), parts.dtype)]
        + [pltpu.SemaphoreType.DMA(())] + gather_sems(count) + [sems] * 6,
        compiler_params=pltpu.CompilerParams(
            collective_id=collective_id, has_side_effects=True, vmem_limit_bytes=VMEM_LIMIT),
    )(parts, targets)


def on_device(sources, targets, enc_weight, dec_weight, active):
    layer_count = dec_weight.shape[1]
    target_pos = lax.axis_index("layer")
    rows, width = sources.shape[1:]
    feat = lax.axis_size("feat")
    tokens = rows * feat
    source_full = gather_call(sources[0], "feat", False, 0).reshape(tokens, width)
    pre_acts = jnp.einsum(
        "fd,td->ft", enc_weight[0], source_full, preferred_element_type=jnp.float32
    )
    mask = active[0].astype(jnp.float32)
    features = (mask * pre_acts).astype(jnp.bfloat16)
    all_features = gather_call(features, "layer", True, 1)
    causal = (jnp.arange(layer_count, dtype=jnp.int32) <= target_pos)[:, None, None]
    masked = jnp.where(causal, all_features, jnp.zeros((), jnp.bfloat16))
    recon = jnp.einsum(
        "lft,lfd->td", masked, dec_weight[0], preferred_element_type=jnp.float32
    ).astype(jnp.bfloat16)
    errors, scaled = reduce_call(
        recon.reshape(feat, rows, width), targets[0], "feat", 1.0 / math.sqrt(tokens), 2
    )
    scaled_full = scaled.reshape(tokens, width)
    partial_grad = jnp.einsum(
        "lfd,td->lft", dec_weight[0], scaled_full, preferred_element_type=jnp.float32
    )
    partial_grad = jnp.where(causal, partial_grad, 0.0).astype(jnp.bfloat16)
    feature_grad = lax.psum_scatter(partial_grad, "layer", scatter_dimension=0, tiled=True)
    grad_dec = jnp.einsum(
        "lft,td->lfd", masked, scaled_full, preferred_element_type=jnp.float32
    ).astype(jnp.bfloat16)
    pre_grad = (mask * feature_grad[0].astype(jnp.float32)).astype(jnp.bfloat16)
    grad_enc = jnp.einsum(
        "ft,td->fd", pre_grad, source_full, preferred_element_type=jnp.float32
    ).astype(jnp.bfloat16)
    return (errors[None], grad_dec[None], grad_enc[None])


def solution(mesh):
    in_specs = (
        P("layer", "feat", None),
        P("layer", "feat", None),
        P("layer", "feat", None),
        P("layer", None, "feat", None),
        P("layer", "feat", None),
    )
    out_specs = (P("layer", "feat", None), P("layer", None, "feat", None), P("layer", "feat", None))
    return jax.shard_map(
        on_device, mesh=mesh, in_specs=in_specs, out_specs=out_specs, check_vma=False
    )
```

time: 490 us -> 310 us (0.63)
  waiting for transfers between devices: 378 us -> 17.8 us
  Pallas kernels: 0 us -> 184 us
    all_gather x3 -> x0, waiting for transfers between devices: 184 us -> none  [the longest x1 78.3 us: on_device(): source_full = lax.all_gather(sources, 'feat', axis=1, tiled=True)]
    pallas_call x0 -> x3, Pallas kernels: none -> 184 us  [the longest x1 97.3 us: reduce_call(): pl.pallas_call(functools.partial(reduce_kernel, axis, count, scale), out_...]
    reduce_scatter x1 -> x0, waiting for transfers between devices: 149 us -> none  [on_device(): lax.psum_scatter(recon_terms, 'feat', scatter_dimension=1, tiled=True)]
    reduce_scatter x1, waiting for transfers between devices: 44.8 us -> 17.8 us  [on_device(): lax.psum_scatter(partial_grad, 'layer', scatter_dimension=0, tiled=True)]
  transfers between devices with their start and end apart: 5 -> 1, of which waited for: 5 -> 1; matrix products, arithmetic and copies ran while one was open for 5% -> 8% of each run, Pallas kernels for 0% -> 0%
where the time goes in v1:
time: 310 us
  Pallas kernels  184 us (59%)
  matrix products  91.2 us (29%)
  waiting for transfers between devices  17.8 us (6%)
  between operations  14.1 us (5%)
    pallas_call x1, Pallas kernels, reduce_call(): pl.pallas_call(functools.partial(reduce_kernel, axis, count, scale), out_...  97.3 us
    pallas_call x2, Pallas kernels, gather_call(): pl.pallas_call(functools.partial(gather_kernel, axis, count, causal), out...  86.2 us
    dot_general x1, matrix products, on_device(): jnp.einsum('lft,td->lfd', masked, scaled_full, preferred_element_type=jnp...  25.2 us
    dot_general x1, matrix products, on_device(): jnp.einsum('lft,lfd->td', masked, dec_weight[0], preferred_element_type=j...  23.1 us
    dot_general x1, matrix products, on_device(): jnp.einsum('lfd,td->lft', dec_weight[0], scaled_full, preferred_element_t...  22.5 us
    reduce_scatter x1, waiting for transfers between devices, on_device(): lax.psum_scatter(partial_grad, 'layer', scatter_dimension=0, tiled=True)  17.8 us
    dot_general x1, matrix products, on_device(): jnp.einsum('ft,td->fd', pre_grad, source_full, preferred_element_type=jnp...  10.4 us
    dot_general x1, matrix products, on_device(): jnp.einsum('fd,td->ft', enc_weight[0], source_full, preferred_element_typ...  10.1 us
  transfers between devices with their start and end apart: 1, of which 1 were waited for; matrix products, arithmetic and copies ran while one was open for 8% of the time, Pallas kernels for 0%

profile of v1, /device:TPU:0, one launch (start us, length us, event | category | flops | bytes accessed | tf_op | source)
XLA Modules:
  0.0 309.7 jit_solution(3352407095218746471)
XLA Ops:
  7.2 0.0 copy-start.2
  7.2 0.0 reduce-scatter.2.cloned.1.call-start
  7.2 53.2 %shard_map.76 = bf16[8,64,4096]{2,1,0:T(8,128)(2,1)} custom-call(bf16[64,4096]{1,0:T(8,128)(2,1)} %bitcast.48), custom_call_target="tpu_custom_call" | custom-call | tf_op jit(solution)/shard_map/pallas_call | solution.py:112
  60.5 0.0 copy-done.2
  60.5 10.1 %fusion.9.own = bf16[1024,512]{1,0:T(8,128)(2,1)} fusion(s32[1,1024,512]{2,1,0:T(8,128)S(1)} %copy-done.2, bf16[512,4096]{1,0:T(8,128)(2,1)} %bitcast.46, bf16[1,1024,4096]{2,1,0:T(8,128)(2,1)} %param.7), kind=kOutput, calls=%fused_computation.13 | convolution fusion | flops 4296540160 | bytes 15728640 | tf_op jit(solution)/shard_map/fd,td->ft/dot_general | solution.py:251
  70.5 33.0 %shard_map.77 = bf16[4,1024,512]{2,1,0:T(8,128)(2,1)} custom-call(bf16[1024,512]{1,0:T(8,128)(2,1)} %fusion.9.own), custom_call_target="tpu_custom_call" | custom-call | tf_op jit(solution)/shard_map/pallas_call | solution.py:112
  103.5 0.0 copy-start
  103.5 23.1 %bitcast_convert_fusion = bf16[512,4096]{1,0:T(8,128)(2,1)S(1)} fusion(bf16[1,4,1024,4096]{3,2,1,0:T(8,128)(2,1)} %param.8, bf16[4,1024,512]{2,1,0:T(8,128)(2,1)} %shard_map.77, pred[4]{0:T(512)(128)(4,1)S(1)} %iota_compare_fusion), kind=kOutput, calls=%fused_computation.5 | convolution fusion | flops 17184063488 | bytes 41943044 | tf_op jit(solution)/shard_map/lft,lfd->td/dot_general | solution.py:259
  126.6 0.0 copy-done
  126.6 97.3 %shard_map.78 = (f32[64,4096]{1,0:T(8,128)S(1)}, bf16[8,64,4096]{2,1,0:T(8,128)(2,1)S(1)}) custom-call(bf16[8,64,4096]{2,1,0:T(8,128)(2,1)S(1)} %bitcast.41, bf16[64,4096]{1,0:T(8,128)(2,1)S(1)} %bitcast.43), custom_call_target="tpu_custom_call" | custom-call | tf_op jit(solution)/shard_map/pallas_call | solution.py:229
  223.9 0.0 copy-start.1
  224.0 2.0 copy-done.1
  226.0 22.5 %fusion.8 = bf16[4,1024,512]{2,1,0:T(8,128)(2,1)} fusion(pred[4]{0:T(512)(128)(4,1)S(1)} %iota_compare_fusion, bf16[512,4096,1]{1,0,2:T(8,128)(2,1)S(1)} %bitcast.44, bf16[1,4,1024,4096]{3,2,1,0:T(8,128)(2,1)} %param.8), kind=kOutput, calls=%fused_computation.10 | convolution fusion | flops 17181966336 | bytes 41943044 | tf_op jit(solution)/shard_map/lfd,td->lft/dot_general | solution.py:266
  248.4 0.0 reduce-scatter.2.cloned.1.call-update
  248.5 25.2 %convert_bitcast_fusion = bf16[1,4,1024,4096]{3,2,1,0:T(8,128)(2,1)} fusion(bf16[512,4096,1]{1,0,2:T(8,128)(2,1)} %bitcast.45, bf16[4,1024,512]{2,1,0:T(8,128)(2,1)} %shard_map.77, pred[4]{0:T(512)(128)(4,1)S(1)} %iota_compare_fusion), kind=kOutput, calls=%fused_computation.4 | convolution fusion | flops 17198743552 | bytes 41943044 | tf_op jit(solution)/shard_map/lft,td->lfd/dot_general | solution.py:271
  273.7 17.8 %reduce-scatter.2.cloned.1.call-done = bf16[1,1024,512]{2,1,0:T(8,128)(2,1)} async-done(((bf16[4,1024,512]{2,1,0:T(8,128)(2,1)}), bf16[1,1024,512]{2,1,0:T(8,128)(2,1)}) %reduce-scatter.2.cloned.1.call-update) | async-done | bytes 1048592 | tf_op jit(solution)/shard_map/reduce_scatter | solution.py:270
  291.4 10.4 %convert_bitcast_fusion.1 = bf16[1,1024,4096]{2,1,0:T(8,128)(2,1)} fusion(bf16[512,4096]{1,0:T(8,128)(2,1)} %bitcast.47, bf16[1,1024,512]{2,1,0:T(8,128)(2,1)} %reduce-scatter.2.cloned.1.call-done, s32[1,1024,512]{2,1,0:T(8,128)S(1)} %copy-done.2), kind=kOutput, calls=%fused_computation.8 | convolution fusion | flops 4301258752 | bytes 15728640 | tf_op jit(solution)/shard_map/ft,td->fd/dot_general | solution.py:275
  301.8 1.0 copy.13
  (1 shorter events, 0.0 us)
Async XLA Ops:
  7.2 53.3 %copy-start.2 = (s32[1,1024,512]{2,1,0:T(8,128)S(1)}, s32[1,1024,512]{2,1,0:T(8,128)}, u32[]{:S(2)}) copy-start(s32[1,1024,512]{2,1,0:T(8,128)} %param.9) | copy-start | bytes 6291460
  7.2 284.2 %reduce-scatter.2.cloned.1.call-start = ((), (), s32[]{:S(2)}) async-start(), calls=%async_computation.1 | async-start | bytes 5242880 | tf_op jit(solution)/shard_map/reduce_scatter | solution.py:270
  103.5 23.1 %copy-start = (bf16[1,64,4096]{2,1,0:T(8,128)(2,1)S(1)}, bf16[1,64,4096]{2,1,0:T(8,128)(2,1)}, u32[]{:S(2)}) copy-start(bf16[1,64,4096]{2,1,0:T(8,128)(2,1)} %param.6) | copy-start | bytes 1572868
  223.9 2.0 copy-start.1
Sparse Core Ops, SparseCore 0:
  248.6 42.7 reduce-scatter.1

commit v2 on v1

--- a/solution.py
+++ b/solution.py
@@ -30,7 +30,7 @@
     pl.semaphore_wait(barrier, 1 + (z > 0).astype(jnp.int32) + (z < length - 1).astype(jnp.int32))
 
 
-def gather(axis, count, causal, own, out, line_sem, side_sem, recv_sem):
+def gather(axis, count, causal, own, out, line_sem, side_sem, recv_sem, work=None):
     me, z, y, length = place(axis, count)
     other = 1 - y
 
@@ -76,10 +76,26 @@
                 pl.when(z > 0)(lambda: left(line, out.at[block]).start())
                 across(line, out.at[block]).start()
 
+        if work is not None:
+            if step == 1:
+                work(z)
+            else:
+                pl.when(z - step + 1 >= 0)(lambda: work(z - step + 1))
+                pl.when(z + step - 1 < length)(lambda: work(z + step - 1))
+
+    if work is not None:
+        last = length - 1
+        if last == 0:
+            work(z)
+        else:
+            pl.when(z - last >= 0)(lambda: work(z - last))
+            pl.when(z + last < length)(lambda: work(z + last))
+
     for line in range(length):
-        @pl.when((line < z) | ((line == z) & (y == 1)) if causal else (z >= 0))
-        def _():
-            arrived(line * 2 + other)
+        if work is None:
+            @pl.when((line < z) | ((line == z) & (y == 1)) if causal else (z >= 0))
+            def _():
+                arrived(line * 2 + other)
 
         @pl.when((line < z) | ((line == z) & (y == 0)) if causal else (z >= 0))
         def _():
@@ -98,25 +114,149 @@
     ]
 
 
-def gather_kernel(axis, count, causal, own, out, local_sem, line_sem, side_sem, recv_sem):
-    me = lax.axis_index(axis)
-    local = pltpu.make_async_copy(own, out.at[me], local_sem)
-    local.start()
-    greet(axis, count)
-    gather(axis, count, causal, own, out, line_sem, side_sem, recv_sem)
-    local.wait()
-
-
-def gather_call(block, axis, causal, collective_id):
-    count = lax.axis_size(axis)
+def encode_kernel(
+    feat_count, layer_count, own, enc_hbm, mask, full_out, features_out,
+    full, enc, features, local_sem, layer_sem, line_sem, side_sem, recv_sem,
+    right_send, across_send, feature_recv,
+):
+    me, z, y, length = place("feat", feat_count)
+    layer, chip, core, chips = place("layer", layer_count)
+    rows, width = own.shape
+    tile = min(256, enc.shape[0])
+    group = 2 if rows % 16 == 0 else 1
+    enc_copy = pltpu.make_async_copy(enc_hbm, enc, local_sem.at[0])
+    enc_copy.start()
+    own_copy = pltpu.make_async_copy(own, full.at[me], local_sem.at[1])
+    own_copy.start()
+
+    barrier = pltpu.get_barrier_semaphore()
+
+    def signal(axis, device):
+        pl.semaphore_signal(barrier, inc=1, device_id={axis: device}, device_id_type=MESH)
+
+    signal("feat", me + 1 - 2 * y)
+    signal("layer", layer + 1 - 2 * core)
+    pl.when(z > 0)(lambda: signal("feat", me - 2))
+    pl.when(z < length - 1)(lambda: signal("feat", me + 2))
+    pl.when(chip > 0)(lambda: signal("layer", layer - 2))
+    pl.when(chip < chips - 1)(lambda: signal("layer", layer + 2))
+    pl.semaphore_wait(
+        barrier,
+        2 + (z > 0).astype(jnp.int32) + (z < length - 1).astype(jnp.int32)
+        + (chip > 0).astype(jnp.int32) + (chip < chips - 1).astype(jnp.int32))
+
+    def send(hop, line, sem, device):
+        block = features.at[layer - 2 * hop, line]
+        return pltpu.make_async_remote_copy(
+            src_ref=block, dst_ref=block, send_sem=sem.at[hop, line],
+            recv_sem=feature_recv.at[layer - 2 * hop, line],
+            device_id={"layer": device}, device_id_type=MESH)
+
+    def right(hop, line):
+        return send(hop, line, right_send, layer + 2)
+
+    def across(hop, line):
+        return send(hop, line, across_send, layer + 1 - 2 * core)
+
+    def landed(source, line):
+        block = features.at[source, line]
+        pltpu.make_async_remote_copy(
+            src_ref=block, dst_ref=block, send_sem=right_send.at[0, line],
+            recv_sem=feature_recv.at[source, line],
+            device_id={"layer": layer}, device_id_type=MESH).wait_recv()
+
+    def relay(line):
+        for hop in range(1, chips):
+            @pl.when(chip >= hop)
+            def _():
+                landed(layer - 2 * hop, line)
+                pl.when(chip < chips - 1)(lambda: right(hop, line).start())
+                across(hop, line).start()
+
+    def work(line):
+        pltpu.make_async_remote_copy(
+            src_ref=own, dst_ref=full.at[line * 2 + 1 - y], send_sem=side_sem.at[0],
+            recv_sem=recv_sem.at[line * 2 + 1 - y],
+            device_id={"feat": me}, device_id_type=MESH).wait_recv()
+
+        @pl.loop(0, enc.shape[0] // tile)
+        def _(index):
+            at = pl.ds(pl.multiple_of(index * tile, tile), tile)
+            for part in range(2 // group):
+                block = full[pl.ds(line * 2 + part, group)].reshape(group * rows, width)
+                acts = lax.dot_general(
+                    block, enc[at, :], (((1,), (1,)), ((), ())),
+                    preferred_element_type=jnp.float32)
+                tokens = pl.ds(part * rows, group * rows)
+                kept = mask[line, tokens, at].astype(jnp.float32) * acts
+                features[layer, line, tokens, at] = kept.astype(features.dtype)
+
+        pl.when(chip < chips - 1)(lambda: right(0, line).start())
+        pl.when(core == 0)(lambda: across(0, line).start())
+
+    enc_copy.wait()
+    own_copy.wait()
+    gather("feat", feat_count, False, own, full, line_sem, side_sem, recv_sem, work)
+    full_copy = pltpu.make_async_copy(full, full_out, local_sem.at[0])
+    full_copy.start()
+    relay(z)
+    for step in range(1, length):
+        pl.when(z - step >= 0)(lambda: relay(z - step))
+        pl.when(z + step < length)(lambda: relay(z + step))
+    for line in range(length):
+        pl.when(core == 1)(lambda: landed(layer - 1, line))
+        for hop in range(1, chips):
+            pl.when(chip >= hop)(lambda: landed(layer - 2 * hop + 1 - 2 * core, line))
+        for hop in range(chips):
+            @pl.when(chip >= hop)
+            def _():
+                pl.when(chip < chips - 1)(lambda: right(hop, line).wait_send())
+                if hop == 0:
+                    pl.when(core == 0)(lambda: across(hop, line).wait_send())
+                else:
+                    across(hop, line).wait_send()
+
+    def out_copy(source):
+        return pltpu.make_async_copy(
+            features.at[source], features_out.at[source], layer_sem.at[source])
+
+    for source in range(layer_count):
+        pl.when(source <= layer)(lambda: out_copy(source).start())
+    for source in range(layer_count):
+        pl.when(source <= layer)(lambda: out_copy(source).wait())
+    full_copy.wait()
+
+
+def encode_call(sources, enc_weight, mask, collective_id):
+    count, layers = lax.axis_size("feat"), lax.axis_size("layer")
+    rows, width = sources.shape
+    size = enc_weight.shape[0]
+    length, chips = count // 2, layers // 2
+    hbm = pl.BlockSpec(memory_space=pl.ANY)
+    full_shape = (count, rows, width)
+    feature_shape = (layers, length, 2 * rows, size)
     return pl.pallas_call(
-        functools.partial(gather_kernel, axis, count, causal),
-        out_shape=jax.ShapeDtypeStruct((count,) + block.shape, block.dtype),
-        in_specs=[pl.BlockSpec(memory_space=pl.ANY)],
-        out_specs=pl.BlockSpec(memory_space=pl.ANY),
-        scratch_shapes=[pltpu.SemaphoreType.DMA(())] + gather_sems(count),
-        compiler_params=pltpu.CompilerParams(collective_id=collective_id, has_side_effects=True),
-    )(block)
+        functools.partial(encode_kernel, count, layers),
+        out_shape=(
+            jax.ShapeDtypeStruct(full_shape, sources.dtype),
+            jax.ShapeDtypeStruct(feature_shape, sources.dtype),
+        ),
+        in_specs=[hbm, hbm, pl.BlockSpec(memory_space=pltpu.VMEM)],
+        out_specs=(hbm, hbm),
+        scratch_shapes=[
+            pltpu.VMEM(full_shape, sources.dtype),
+            pltpu.VMEM(enc_weight.shape, sources.dtype),
+            pltpu.VMEM(feature_shape, sources.dtype),
+            pltpu.SemaphoreType.DMA((2,)),
+            pltpu.SemaphoreType.DMA((layers,)),
+        ] + gather_sems(count) + [
+            pltpu.SemaphoreType.DMA((chips, length)),
+            pltpu.SemaphoreType.DMA((chips, length)),
+            pltpu.SemaphoreType.DMA((layers, length)),
+        ],
+        compiler_params=pltpu.CompilerParams(
+            collective_id=collective_id, has_side_effects=True, vmem_limit_bytes=VMEM_LIMIT),
+    )(sources, enc_weight, mask.reshape(length, 2 * rows, size))
 
 
 def reduce_kernel(
@@ -241,39 +381,53 @@
     )(parts, targets)
 
 
+def scatter_layers(partial):
+    layers = lax.axis_size("layer")
+    layer, chip, core, chips = place("layer", layers)
+    pairs = partial.reshape((chips, 2) + partial.shape[1:])
+    swap = [(device, device ^ 1) for device in range(layers)]
+    given = lax.ppermute(lax.dynamic_index_in_dim(pairs, 1 - core, 1, keepdims=False), "layer", swap)
+    kept = lax.dynamic_index_in_dim(pairs, core, 1, keepdims=False)
+    sums = (kept.astype(jnp.float32) + given.astype(jnp.float32)).astype(partial.dtype)
+    total = lax.dynamic_index_in_dim(sums, chip, 0, keepdims=False).astype(jnp.float32)
+    for shift in range(1, chips):
+        target = lax.rem(chip + shift, chips)
+        moves = [(device, (device + 2 * shift) % layers) for device in range(layers)]
+        sent = lax.dynamic_index_in_dim(sums, target, 0, keepdims=False)
+        total += lax.ppermute(sent, "layer", moves).astype(jnp.float32)
+    return total
+
+
 def on_device(sources, targets, enc_weight, dec_weight, active):
     layer_count = dec_weight.shape[1]
     target_pos = lax.axis_index("layer")
     rows, width = sources.shape[1:]
     feat = lax.axis_size("feat")
     tokens = rows * feat
-    source_full = gather_call(sources[0], "feat", False, 0).reshape(tokens, width)
-    pre_acts = jnp.einsum(
-        "fd,td->ft", enc_weight[0], source_full, preferred_element_type=jnp.float32
-    )
-    mask = active[0].astype(jnp.float32)
-    features = (mask * pre_acts).astype(jnp.bfloat16)
-    all_features = gather_call(features, "layer", True, 1)
+    mask = active[0].astype(jnp.bfloat16).T
+    source_full, all_features = encode_call(sources[0], enc_weight[0], mask, 0)
+    source_full = source_full.reshape(tokens, width)
+    all_features = all_features.reshape(layer_count, tokens, -1)
     causal = (jnp.arange(layer_count, dtype=jnp.int32) <= target_pos)[:, None, None]
     masked = jnp.where(causal, all_features, jnp.zeros((), jnp.bfloat16))
     recon = jnp.einsum(
-        "lft,lfd->td", masked, dec_weight[0], preferred_element_type=jnp.float32
+        "ltf,lfd->td", masked, dec_weight[0], preferred_element_type=jnp.float32
     ).astype(jnp.bfloat16)
     errors, scaled = reduce_call(
         recon.reshape(feat, rows, width), targets[0], "feat", 1.0 / math.sqrt(tokens), 2
     )
     scaled_full = scaled.reshape(tokens, width)
     partial_grad = jnp.einsum(
-        "lfd,td->lft", dec_weight[0], scaled_full, preferred_element_type=jnp.float32
+        "lfd,td->ltf", dec_weight[0], scaled_full, preferred_element_type=jnp.float32
     )
     partial_grad = jnp.where(causal, partial_grad, 0.0).astype(jnp.bfloat16)
-    feature_grad = lax.psum_scatter(partial_grad, "layer", scatter_dimension=0, tiled=True)
+    feature_grad = scatter_layers(partial_grad)
     grad_dec = jnp.einsum(
-        "lft,td->lfd", masked, scaled_full, preferred_element_type=jnp.float32
+        "ltf,td->lfd", masked, scaled_full, preferred_element_type=jnp.float32
     ).astype(jnp.bfloat16)
-    pre_grad = (mask * feature_grad[0].astype(jnp.float32)).astype(jnp.bfloat16)
+    pre_grad = (mask.astype(jnp.float32) * feature_grad).astype(jnp.bfloat16)
     grad_enc = jnp.einsum(
-        "ft,td->fd", pre_grad, source_full, preferred_element_type=jnp.float32
+        "tf,td->fd", pre_grad, source_full, preferred_element_type=jnp.float32
     ).astype(jnp.bfloat16)
     return (errors[None], grad_dec[None], grad_enc[None])
 

time: 310 us -> 285 us (0.919)
  Pallas kernels: 184 us -> 160 us
  local copies, waits for them, and re-layouts: 2.99 us -> 19.4 us
  waiting for transfers between devices: 17.8 us -> 2.29 us
  starting transfers between devices: 0.04 us -> 14.9 us
  between operations: 14.1 us -> 0.78 us
  matrix products: 91.2 us -> 79.7 us
  other arithmetic: 0.01 us -> 7.5 us
    pallas_call x2 -> x1, Pallas kernels: 86.2 us -> 63 us  [encode_call(): pl.pallas_call(functools.partial(encode_kernel, count, layers), out_shape...]
    reduce_scatter x1 -> x0, waiting for transfers between devices: 17.8 us -> none  [on_device(): lax.psum_scatter(partial_grad, 'layer', scatter_dimension=0, tiled=True)]
    ppermute x0 -> x2, starting transfers between devices: none -> 14.9 us  [the longest x1 14.9 us: scatter_layers(): total += lax.ppermute(sent, 'layer', moves).astype(jnp.float32)]
    dot_general x5 -> x4, matrix products: 91.2 us -> 79.7 us  [the longest x1 24.4 us: on_device(): jnp.einsum('ltf,lfd->td', masked, dec_weight[0], preferred_element_type=j...]
    dynamic_slice x0 -> x2, local copies, waits for them, and re-layouts: none -> 8.19 us  [the longest x1 4.25 us: scatter_layers(): kept = lax.dynamic_index_in_dim(pairs, core, 1, keepdims=False)]
    unnamed x7 -> x18, local copies, waits for them, and re-layouts: 2.99 us -> 9.65 us
    select_n x0 -> x2, other arithmetic: none -> 3.22 us  [on_device(): masked = jnp.where(causal, all_features, jnp.zeros((), jnp.bfloat16))]
  transfers between devices with their start and end apart: 1 -> 2, of which waited for: 1 -> 1; matrix products, arithmetic and copies ran while one was open for 8% -> 10% of each run, Pallas kernels for 0% -> 0%
where the time goes in v2:
time: 285 us; the launch traced here: 284 us
  Pallas kernels  160 us (56%)
  matrix products  79.7 us (28%)
  local copies, waits for them, and re-layouts  19.4 us (7%)
  starting transfers between devices  14.9 us (5%)
  other arithmetic  7.5 us (3%)
    pallas_call x1, Pallas kernels, reduce_call(): pl.pallas_call(functools.partial(reduce_kernel, axis, count, scale), out_...  96.8 us
    pallas_call x1, Pallas kernels, encode_call(): pl.pallas_call(functools.partial(encode_kernel, count, layers), out_shape...  63 us
    dot_general x1, matrix products, on_device(): jnp.einsum('ltf,lfd->td', masked, dec_weight[0], preferred_element_type=j...  24.4 us
    dot_general x1, matrix products, on_device(): jnp.einsum('lfd,td->ltf', dec_weight[0], scaled_full, preferred_element_t...  22.6 us
    dot_general x1, matrix products, on_device(): jnp.einsum('ltf,td->lfd', masked, scaled_full, preferred_element_type=jnp...  21.9 us
    ppermute x1, starting transfers between devices, scatter_layers(): total += lax.ppermute(sent, 'layer', moves).astype(jnp.float32)  14.9 us
    dot_general x1, matrix products, on_device(): jnp.einsum('tf,td->fd', pre_grad, source_full, preferred_element_type=jnp...  10.8 us
    unnamed x18, local copies, waits for them, and re-layouts  9.65 us
  transfers between devices with their start and end apart: 2, of which 1 were waited for; matrix products, arithmetic and copies ran while one was open for 10% of the time, Pallas kernels for 0%

profile of v2, /device:TPU:0, one launch (start us, length us, event | category | flops | bytes accessed | tf_op | source)
XLA Modules:
  0.0 284.4 jit_solution(12662700280117586756)
XLA Ops:
  0.6 0.0 copy-start.1
  0.7 1.9 convert_bitcast_fusion.2
  2.6 0.0 copy-start.7
  2.6 0.5 copy.8
  3.1 63.0 %shard_map.76 = (bf16[8,64,4096]{2,1,0:T(8,128)(2,1)S(1)}, bf16[4,4,128,1024]{3,2,1,0:T(8,128)(2,1)S(1)}) custom-call(bf16[64,4096]{1,0:T(8,128)(2,1)S(1)} %bitcast.55, bf16[1024,4096]{1,0:T(8,128)(2,1)} %bitcast.60, bf16[4,128,1024]{2,1,0:T(8,128)(2,1)S(1)} %bitcast.52), custom_call_target="tpu_custom_call" | custom-call | tf_op jit(solution)/shard_map/pallas_call | solution.py:238
  66.2 0.0 copy-done.7
  66.2 0.0 copy-start.3
  66.2 1.9 copy-done.3
  68.1 2.0 copy-done
  70.2 0.5 bitcast_select_fusion
  70.7 0.0 copy-start.2
  70.7 24.4 %bitcast_convert_fusion = bf16[512,4096]{1,0:T(8,128)(2,1)S(1)} fusion(bf16[4,512,1024]{2,1,0:T(8,128)(2,1)S(1)} %bitcast_select_fusion, bf16[1,4,1024,4096]{3,2,1,0:T(8,128)(2,1)} %param.8), kind=kOutput, calls=%fused_computation.5 | convolution fusion | flops 17181966336 | bytes 41943040 | tf_op jit(solution)/shard_map/ltf,lfd->td/dot_general | solution.py:413
  95.2 0.0 copy-done.2
  95.2 96.8 %shard_map.77 = (f32[64,4096]{1,0:T(8,128)S(1)}, bf16[8,64,4096]{2,1,0:T(8,128)(2,1)S(1)}) custom-call(bf16[8,64,4096]{2,1,0:T(8,128)(2,1)S(1)} %bitcast.53, bf16[64,4096]{1,0:T(8,128)(2,1)S(1)} %bitcast.56), custom_call_target="tpu_custom_call" | custom-call | tf_op jit(solution)/shard_map/pallas_call | solution.py:369
  192.0 0.0 copy-start.4
  192.0 2.0 copy-done.4
  194.0 22.6 %select_convert_fusion = bf16[512,4,1024]{2,0,1:T(8,128)(2,1)} fusion(pred[4]{0:T(512)(128)(4,1)S(1)} %iota_compare_fusion, bf16[512,4096,1]{1,0,2:T(8,128)(2,1)S(1)} %bitcast.58, bf16[1,4,1024,4096]{3,2,1,0:T(8,128)(2,1)} %param.8), kind=kOutput, calls=%fused_computation.7 | convolution fusion | flops 17181966336 | bytes 41943044 | tf_op jit(solution)/shard_map/lfd,td->ltf/dot_general | solution.py:420
  216.6 4.3 %constant_dynamic-slice_fusion.1 = (bf16[2,1,512,1024]{3,2,1,0:T(8,128)(2,1)S(1)}, bf16[2,1,512,1024]{3,2,1,0:T(8,128)(2,1)}) fusion(bf16[2,2,512,1024]{3,2,1,0:T(8,128)(2,1)} %bitcast.62, s32[]{:T(128)S(6)} %select_n.37, s32[]{:T(128)S(6)} %select_n.38), kind=kLoop, calls=%fused_computation.21 | loop fusion | bytes 8388616 | tf_op jit(solution)/shard_map/jit(dynamic_index_in_dim)/dynamic_slice | solution.py:390
  220.9 3.9 %copy.11 = bf16[2,1,512,1024]{2,3,0,1:T(8,128)(2,1)} copy(bf16[2,1,512,1024]{3,2,1,0:T(8,128)(2,1)} %get-tuple-element.12) | data formatting | bytes 4194304 | tf_op jit(solution)/shard_map/jit(dynamic_index_in_dim)/dynamic_slice | solution.py:389
  224.8 0.0 collective-permute-start
  224.8 2.6 copy.13
  227.4 2.7 broadcast_select_fusion
  230.0 0.0 copy-start.5
  230.1 0.0 collective-permute-done
  230.1 0.1 copy-done.6
  230.2 2.4 fusion.6
  232.6 1.0 dynamic-slice_bitcast_fusion
  233.6 14.9 %collective-permute-start.1 = (bf16[512,1024]{0,1:T(8,128)(2,1)}, bf16[512,1024]{0,1:T(8,128)(2,1)}, u32[]{:S(2)}, u32[]{:S(2)}) collective-permute-start(bf16[512,1024]{0,1:T(8,128)(2,1)} %dynamic-slice_bitcast_fusion), channel_id=1, source_target_pairs={{0,16},{8,24},{16,0},{24,8},{1,17},{9,25},{17,1},{25,9},{2,18},{10... | collective-permute-start | bytes 3145736 | tf_op jit(solution)/shard_map/ppermute | solution.py:397
  248.6 21.9 %convert_bitcast_fusion = bf16[1,4,1024,4096]{3,2,1,0:T(8,128)(2,1)} fusion(bf16[4,512,1024]{2,1,0:T(8,128)(2,1)S(1)} %bitcast.61, bf16[512,4096,1]{1,0,2:T(8,128)(2,1)S(1)} %bitcast.59), kind=kOutput, calls=%fused_computation.4 | convolution fusion | flops 17196646400 | bytes 41943040 | tf_op jit(solution)/shard_map/ltf,td->lfd/dot_general | solution.py:425
  270.4 2.3 collective-permute-done.1
  272.7 10.8 %convert_bitcast_fusion.1 = bf16[1,1024,4096]{2,1,0:T(8,128)(2,1)} fusion(bf16[512,4096]{1,0:T(8,128)(2,1)} %bitcast.57, bf16[512,1024]{0,1:T(8,128)(2,1)} %collective-permute-done.1, bf16[512,1024]{0,1:T(8,128)(2,1)} %copy-done.7, bf16[2,512,1024]{1,2,0:T(8,128)(2,1)S(1)} %fusion.6, s32[]{:T(128)S(6)} %select_n.40), kind=kOutput, calls=%fused_computation.6 | convolution fusion | flops 4302307328 | bytes 15728644 | tf_op jit(solution)/shard_map/tf,td->fd/dot_general | solution.py:429
  283.5 1.0 copy.15
  (5 shorter events, 0.0 us)
Async XLA Ops:
  0.6 2.5 copy-start.1
  2.6 63.6 %copy-start.7 = (bf16[512,1024]{0,1:T(8,128)(2,1)}, bf16[512,1024]{0,1:T(8,128)(2,1)S(1)}, u32[]{:S(2)}) copy-start(bf16[512,1024]{0,1:T(8,128)(2,1)S(1)} %convert_bitcast_fusion.2) | copy-start | bytes 3145732
  66.2 2.0 copy-start.3
  68.1 2.0 copy-start
  70.7 24.5 %copy-start.2 = (bf16[1,64,4096]{2,1,0:T(8,128)(2,1)S(1)}, bf16[1,64,4096]{2,1,0:T(8,128)(2,1)}, u32[]{:S(2)}) copy-start(bf16[1,64,4096]{2,1,0:T(8,128)(2,1)} %param.6) | copy-start | bytes 1572868
  192.0 2.0 copy-start.4
  224.8 5.3 %collective-permute-start = (bf16[2,512,1024]{1,2,0:T(8,128)(2,1)}, bf16[2,512,1024]{1,2,0:T(8,128)(2,1)}, u32[]{:S(2)}, u32[]{:S(2)}) collective-permute-start(bf16[2,512,1024]{1,2,0:T(8,128)(2,1)} %bitcast.63), channel_id=1, source_target_pairs={{0,8},{8,0},{16,24},{24,16},{1,9},{9,1},{17,25},{25,17},{2,10},{10... | collective-permute-start | bytes 6291464 | tf_op jit(solution)/shard_map/ppermute | solution.py:389
  227.4 2.9 %copy-start.6 = (bf16[2,1,512,1024]{2,3,0,1:T(8,128)(2,1)S(1)}, bf16[2,1,512,1024]{2,3,0,1:T(8,128)(2,1)}, u32[]{:S(2)}) copy-start(bf16[2,1,512,1024]{2,3,0,1:T(8,128)(2,1)} %copy.13) | copy-start | bytes 6291460
  230.0 18.5 %copy-start.5 = (bf16[8,64,4096]{2,1,0:T(8,128)(2,1)S(1)}, bf16[8,64,4096]{2,1,0:T(8,128)(2,1)}, u32[]{:S(2)}) copy-start(bf16[8,64,4096]{2,1,0:T(8,128)(2,1)} %copy-done.4) | copy-start | bytes 12582916
  233.6 39.1 %collective-permute-start.1 = (bf16[512,1024]{0,1:T(8,128)(2,1)}, bf16[512,1024]{0,1:T(8,128)(2,1)}, u32[]{:S(2)}, u32[]{:S(2)}) collective-permute-start(bf16[512,1024]{0,1:T(8,128)(2,1)} %dynamic-slice_bitcast_fusion), channel_id=1, source_target_pairs={{0,16},{8,24},{16,0},{24,8},{1,17},{9,25},{17,1},{25,9},{2,18},{10... | collective-permute-start | bytes 3145736 | tf_op jit(solution)/shard_map/ppermute | solution.py:397

commit v3 on v2

--- a/solution.py
+++ b/solution.py
@@ -9,7 +9,7 @@
 from jax.sharding import PartitionSpec as P
 
 MESH = pl.DeviceIdType.MESH
-VMEM_LIMIT = 40 * 1024 * 1024
+VMEM_LIMIT = 56 * 1024 * 1024
 
 
 def place(axis, count):
@@ -174,6 +174,11 @@
                 across(hop, line).start()
 
     def work(line):
+        @pl.when(line == z)
+        def _():
+            enc_copy.wait()
+            own_copy.wait()
+
         pltpu.make_async_remote_copy(
             src_ref=own, dst_ref=full.at[line * 2 + 1 - y], send_sem=side_sem.at[0],
             recv_sem=recv_sem.at[line * 2 + 1 - y],
@@ -194,8 +199,11 @@
         pl.when(chip < chips - 1)(lambda: right(0, line).start())
         pl.when(core == 0)(lambda: across(0, line).start())
 
-    enc_copy.wait()
-    own_copy.wait()
+    for source in range(layer_count):
+        @pl.when(source > layer)
+        def _():
+            features[source] = jnp.zeros(features.shape[1:], features.dtype)
+
     gather("feat", feat_count, False, own, full, line_sem, side_sem, recv_sem, work)
     full_copy = pltpu.make_async_copy(full, full_out, local_sem.at[0])
     full_copy.start()
@@ -221,9 +229,9 @@
             features.at[source], features_out.at[source], layer_sem.at[source])
 
     for source in range(layer_count):
-        pl.when(source <= layer)(lambda: out_copy(source).start())
+        out_copy(source).start()
     for source in range(layer_count):
-        pl.when(source <= layer)(lambda: out_copy(source).wait())
+        out_copy(source).wait()
     full_copy.wait()
 
 
@@ -409,25 +417,24 @@
     source_full = source_full.reshape(tokens, width)
     all_features = all_features.reshape(layer_count, tokens, -1)
     causal = (jnp.arange(layer_count, dtype=jnp.int32) <= target_pos)[:, None, None]
-    masked = jnp.where(causal, all_features, jnp.zeros((), jnp.bfloat16))
     recon = jnp.einsum(
-        "ltf,lfd->td", masked, dec_weight[0], preferred_element_type=jnp.float32
+        "ltf,lfd->td", all_features, dec_weight[0], preferred_element_type=jnp.float32
     ).astype(jnp.bfloat16)
     errors, scaled = reduce_call(
         recon.reshape(feat, rows, width), targets[0], "feat", 1.0 / math.sqrt(tokens), 2
     )
     scaled_full = scaled.reshape(tokens, width)
     partial_grad = jnp.einsum(
-        "lfd,td->ltf", dec_weight[0], scaled_full, preferred_element_type=jnp.float32
+        "lfd,td->lft", dec_weight[0], scaled_full, preferred_element_type=jnp.float32
     )
     partial_grad = jnp.where(causal, partial_grad, 0.0).astype(jnp.bfloat16)
     feature_grad = scatter_layers(partial_grad)
     grad_dec = jnp.einsum(
-        "ltf,td->lfd", masked, scaled_full, preferred_element_type=jnp.float32
+        "ltf,td->lfd", all_features, scaled_full, preferred_element_type=jnp.float32
     ).astype(jnp.bfloat16)
-    pre_grad = (mask.astype(jnp.float32) * feature_grad).astype(jnp.bfloat16)
+    pre_grad = (active[0].astype(jnp.float32) * feature_grad).astype(jnp.bfloat16)
     grad_enc = jnp.einsum(
-        "tf,td->fd", pre_grad, source_full, preferred_element_type=jnp.float32
+        "ft,td->fd", pre_grad, source_full, preferred_element_type=jnp.float32
     ).astype(jnp.bfloat16)
     return (errors[None], grad_dec[None], grad_enc[None])
 

time: 285 us -> 284 us (level)
  local copies, waits for them, and re-layouts: 19.4 us -> 13.1 us
  Pallas kernels: 160 us -> 165 us
  matrix products: 79.7 us -> 83.4 us
    unnamed x18 -> x8, local copies, waits for them, and re-layouts: 9.65 us -> 3.52 us
    pallas_call x1, Pallas kernels: 96.8 us -> 102 us  [reduce_call(): pl.pallas_call(functools.partial(reduce_kernel, axis, count, scale), out_...]
    dot_general x4, matrix products: 79.7 us -> 83.4 us  [the longest x1 26.5 us: on_device(): jnp.einsum('ltf,lfd->td', all_features, dec_weight[0], preferred_element_...]
    select_n x2 -> x0, other arithmetic: 3.22 us -> none  [on_device(): masked = jnp.where(causal, all_features, jnp.zeros((), jnp.bfloat16))]
  transfers between devices with their start and end apart: 2 -> 2, of which waited for: 1 -> 2; matrix products, arithmetic and copies ran while one was open for 10% -> 9% of each run, Pallas kernels for 0% -> 0%
where the time goes in v3:
time: 284 us
  Pallas kernels  165 us (58%)
  matrix products  83.4 us (29%)
  local copies, waits for them, and re-layouts  13.1 us (5%)
  starting transfers between devices  13.1 us (5%)
  other arithmetic  5.18 us (2%)
  waiting for transfers between devices  3.87 us (1%)
    pallas_call x1, Pallas kernels, reduce_call(): pl.pallas_call(functools.partial(reduce_kernel, axis, count, scale), out_...  102 us
    pallas_call x1, Pallas kernels, encode_call(): pl.pallas_call(functools.partial(encode_kernel, count, layers), out_shape...  63.2 us
    dot_general x1, matrix products, on_device(): jnp.einsum('ltf,lfd->td', all_features, dec_weight[0], preferred_element_...  26.5 us
    dot_general x1, matrix products, on_device(): jnp.einsum('lfd,td->lft', dec_weight[0], scaled_full, preferred_element_t...  23.8 us
    dot_general x1, matrix products, on_device(): jnp.einsum('ltf,td->lfd', all_features, scaled_full, preferred_element_ty...  21.9 us
    ppermute x1, starting transfers between devices, scatter_layers(): total += lax.ppermute(sent, 'layer', moves).astype(jnp.float32)  13.1 us
    dot_general x1, matrix products, on_device(): jnp.einsum('ft,td->fd', pre_grad, source_full, preferred_element_type=jnp...  11.1 us
  transfers between devices with their start and end apart: 2, of which 2 were waited for; matrix products, arithmetic and copies ran while one was open for 9% of the time, Pallas kernels for 0%

profile of v3, /device:TPU:0, one launch (start us, length us, event | category | flops | bytes accessed | tf_op | source)
XLA Modules:
  0.0 284.1 jit_solution(7938560333746880390)
XLA Ops:
  0.7 1.9 convert_bitcast_fusion.2
  2.5 1.3 copy.8
  3.8 63.2 %shard_map.76 = (bf16[8,64,4096]{2,1,0:T(8,128)(2,1)}, bf16[4,4,128,1024]{3,2,1,0:T(8,128)(2,1)}) custom-call(bf16[64,4096]{1,0:T(8,128)(2,1)} %bitcast.59, bf16[1024,4096]{1,0:T(8,128)(2,1)} %bitcast.53, bf16[4,128,1024]{2,1,0:T(8,128)(2,1)} %bitcast.54), custom_call_target="tpu_custom_call" | custom-call | tf_op jit(solution)/shard_map/pallas_call | solution.py:246
  67.0 26.5 %bitcast_convert_fusion = bf16[512,4096]{1,0:T(8,128)(2,1)} fusion(bf16[4,512,1024]{2,1,0:T(8,128)(2,1)} %bitcast.62, bf16[1,4,1024,4096]{3,2,1,0:T(8,128)(2,1)} %param.8), kind=kOutput, calls=%fused_computation.5 | convolution fusion | flops 17181966336 | bytes 41943040 | tf_op jit(solution)/shard_map/ltf,lfd->td/dot_general | solution.py:420
  93.6 101.7 %shard_map.77 = (f32[64,4096]{1,0:T(8,128)}, bf16[8,64,4096]{2,1,0:T(8,128)(2,1)}) custom-call(bf16[8,64,4096]{2,1,0:T(8,128)(2,1)} %bitcast.55, bf16[64,4096]{1,0:T(8,128)(2,1)} %bitcast.60), custom_call_target="tpu_custom_call" | custom-call | tf_op jit(solution)/shard_map/pallas_call | solution.py:377
  195.3 23.8 %select_convert_fusion = bf16[512,4,1024]{2,0,1:T(8,128)(2,1)} fusion(pred[4]{0:T(512)(128)(4,1)S(1)} %iota_compare_fusion, bf16[512,4096,1]{1,0,2:T(8,128)(2,1)} %bitcast.64, bf16[1,4,1024,4096]{3,2,1,0:T(8,128)(2,1)} %param.8), kind=kOutput, calls=%fused_computation.7 | convolution fusion | flops 17181966336 | bytes 41943044 | tf_op jit(solution)/shard_map/lfd,td->lft/dot_general | solution.py:427
  219.1 4.2 %constant_dynamic-slice_fusion.1 = (bf16[2,1,1024,512]{2,3,1,0:T(8,128)(2,1)S(1)}, bf16[2,1,1024,512]{2,3,1,0:T(8,128)(2,1)}) fusion(bf16[2,2,1024,512]{2,3,1,0:T(8,128)(2,1)} %bitcast.56, s32[]{:T(128)S(6)} %select_n.25, s32[]{:T(128)S(6)} %select_n.26), kind=kLoop, calls=%fused_computation.19 | loop fusion | bytes 8388616 | tf_op jit(solution)/shard_map/jit(dynamic_index_in_dim)/dynamic_slice | solution.py:398
  223.3 3.9 %copy.11 = bf16[2,1,1024,512]{3,2,0,1:T(8,128)(2,1)} copy(bf16[2,1,1024,512]{2,3,1,0:T(8,128)(2,1)} %get-tuple-element.12) | data formatting | bytes 4194304 | tf_op jit(solution)/shard_map/jit(dynamic_index_in_dim)/dynamic_slice | solution.py:397
  227.2 0.0 collective-permute-start
  227.2 2.5 copy.13
  229.8 0.0 copy-start.1
  229.8 0.0 copy-start.2
  229.8 2.0 collective-permute-done
  231.7 3.3 %fusion.6 = bf16[2,1024,512]{2,1,0:T(8,128)(2,1)S(1)} fusion(bf16[2,1024,512]{2,1,0:T(8,128)(2,1)} %collective-permute-done, bf16[2,1,1024,512]{3,2,0,1:T(8,128)(2,1)} %copy.13), kind=kLoop, calls=%fused_computation.9 | loop fusion | flops 4194304 | bytes 6291456 | tf_op jit(solution)/shard_map/convert_element_type | solution.py:399
  235.1 0.1 dynamic-slice_bitcast_fusion
  235.1 13.1 %collective-permute-start.1 = (bf16[1024,512]{1,0:T(8,128)(2,1)S(1)}, bf16[1024,512]{1,0:T(8,128)(2,1)}, u32[]{:S(2)}, u32[]{:S(2)}) collective-permute-start(bf16[1024,512]{1,0:T(8,128)(2,1)S(1)} %dynamic-slice_bitcast_fusion), channel_id=1, source_target_pairs={{0,16},{8,24},{16,0},{24,8},{1,17},{9,25},{17,1},{25,9},{2,18},{10... | collective-permute-start | bytes 3145736 | tf_op jit(solution)/shard_map/ppermute | solution.py:405
  248.2 0.0 copy-done.1
  248.2 0.0 copy-done.2
  248.2 21.9 %convert_bitcast_fusion = bf16[1,4,1024,4096]{3,2,1,0:T(8,128)(2,1)} fusion(bf16[4,512,1024]{2,1,0:T(8,128)(2,1)S(1)} %bitcast.63, bf16[512,4096,1]{1,0,2:T(8,128)(2,1)S(1)} %bitcast.65), kind=kOutput, calls=%fused_computation.4 | convolution fusion | flops 17196646400 | bytes 41943040 | tf_op jit(solution)/shard_map/ltf,td->lfd/dot_general | solution.py:432
  270.1 1.9 collective-permute-done.1
  272.0 0.0 copy-start
  272.0 11.1 %convert_bitcast_fusion.1 = bf16[1,1024,4096]{2,1,0:T(8,128)(2,1)} fusion(bf16[512,4096]{1,0:T(8,128)(2,1)} %bitcast.61, bf16[1024,512]{1,0:T(8,128)(2,1)} %collective-permute-done.1, s32[1,1024,512]{2,1,0:T(8,128)} %param.9, bf16[2,1024,512]{2,1,0:T(8,128)(2,1)S(1)} %fusion.6, s32[]{:T(128)S(6)} %select_n.28), kind=kOutput, calls=%fused_computation.6 | convolution fusion | flops 4302307328 | bytes 16777220 | tf_op jit(solution)/shard_map/ft,td->fd/dot_general | solution.py:436
  283.1 0.0 copy-done
  283.2 1.0 copy.15
  (1 shorter events, 0.0 us)
Async XLA Ops:
  227.2 4.5 %collective-permute-start = (bf16[2,1024,512]{2,1,0:T(8,128)(2,1)}, bf16[2,1024,512]{2,1,0:T(8,128)(2,1)}, u32[]{:S(2)}, u32[]{:S(2)}) collective-permute-start(bf16[2,1024,512]{2,1,0:T(8,128)(2,1)} %bitcast.57), channel_id=1, source_target_pairs={{0,8},{8,0},{16,24},{24,16},{1,9},{9,1},{17,25},{25,17},{2,10},{10... | collective-permute-start | bytes 6291464 | tf_op jit(solution)/shard_map/ppermute | solution.py:397
  229.8 18.4 %copy-start.1 = (bf16[4,4,128,1024]{3,2,1,0:T(8,128)(2,1)S(1)}, bf16[4,4,128,1024]{3,2,1,0:T(8,128)(2,1)}, u32[]{:S(2)}) copy-start(bf16[4,4,128,1024]{3,2,1,0:T(8,128)(2,1)} %get-tuple-element.7) | copy-start | bytes 12582916
  229.8 18.4 %copy-start.2 = (bf16[8,64,4096]{2,1,0:T(8,128)(2,1)S(1)}, bf16[8,64,4096]{2,1,0:T(8,128)(2,1)}, u32[]{:S(2)}) copy-start(bf16[8,64,4096]{2,1,0:T(8,128)(2,1)} %get-tuple-element.9) | copy-start | bytes 12582916
  235.1 36.9 %collective-permute-start.1 = (bf16[1024,512]{1,0:T(8,128)(2,1)S(1)}, bf16[1024,512]{1,0:T(8,128)(2,1)}, u32[]{:S(2)}, u32[]{:S(2)}) collective-permute-start(bf16[1024,512]{1,0:T(8,128)(2,1)S(1)} %dynamic-slice_bitcast_fusion), channel_id=1, source_target_pairs={{0,16},{8,24},{16,0},{24,8},{1,17},{9,25},{17,1},{25,9},{2,18},{10... | collective-permute-start | bytes 3145736 | tf_op jit(solution)/shard_map/ppermute | solution.py:405
  272.0 11.1 %copy-start = (f32[64,4096]{1,0:T(8,128)S(1)}, f32[64,4096]{1,0:T(8,128)}, u32[]{:S(2)}) copy-start(f32[64,4096]{1,0:T(8,128)} %get-tuple-element.8) | copy-start | bytes 3145732
